TPU v7x, 32 devices: a whole 2x2x4 slice. The times are simulated.
32 devices in a mesh: state: 8 (over z, x), rank: 4 (over y, core).
Axes of the slice: x: 2, y: 2, z: 4, core: 2. Of those that a mesh axis runs over, the one named last changes fastest.
Arguments:
- token_ids: int32 [3, 128], replicated, may hold values from 0 to 9999
- word_emb: bfloat16 [10000, 128], replicated, may hold values from -6 to 6
- state_emb: bfloat16 [32768, 128], P('state'), may hold values from -3 to 3
- log_norm: float32 [32768], P('state'), may hold values from -0.5 to 1
- beta_last: bfloat16 [32768, 128], P('state'), may hold values from 0.19921875 to 5
- forward_marg: bfloat16 [32768, 384], P('state'), may hold values from 0.049804688 to 2
- trans_left: bfloat16 [32768, 2048], P('state', 'rank'), as said below
- trans_right: bfloat16 [32768, 2048], P('state', 'rank'), as said below
Outputs:
- beta_first: bfloat16 [32768, 128], P('state')
- grad_left: bfloat16 [32768, 2048], P('state', 'rank')
- grad_right: bfloat16 [32768, 2048], P('state', 'rank')
Inputs may be any that keep to these rules, and one draw needn't show every extreme that they name: `trans_left`: positive entries. `trans_right`: positive entries.
All inputs are finite; a program needn't handle non-finite values.
Results may differ from a plain program's by a relative error of at most 0.009.
Values may be sent and summed in bfloat16 or wider, within the bound.
No kernel may reach another device: no remote copies, remote signals or barrier semaphores. Data moves between devices by JAX's collectives and lax.ppermute only.
A program may use at most 128 MiB of HBM per device.

v0:
```python
import jax
import jax.numpy as jnp
from jax import lax
from jax.sharding import PartitionSpec as P


def on_device(
    token_ids, word_emb, state_emb, log_norm, beta_last, forward_marg, trans_left, trans_right
):
    states_all = lax.axis_size("state") * state_emb.shape[0]
    steps = token_ids.shape[0]
    batch = beta_last.shape[1]
    local_columns = jnp.sum(trans_left, axis=0, dtype=jnp.float32)
    fwd_part = lax.dot_general(
        forward_marg, trans_left, (((0,), (0,)), ((), ())), preferred_element_type=jnp.float32
    )
    fwd_proj = (lax.psum(fwd_part, "state") / states_all).astype(jnp.bfloat16)
    beta = beta_last
    weighted_list = []
    proj_list = []
    for step in reversed(range(steps)):
        words = jnp.take(word_emb, token_ids[step], axis=0)
        logits = jnp.dot(state_emb, words.T, preferred_element_type=jnp.float32)
        emit = jnp.exp(logits - log_norm[:, None])
        weighted = (emit * beta.astype(jnp.float32)).astype(jnp.bfloat16)
        proj_part = lax.dot_general(
            weighted, trans_right, (((0,), (0,)), ((), ())), preferred_element_type=jnp.float32
        )
        projb = lax.psum(proj_part, "state").astype(jnp.bfloat16)
        total = lax.psum(jnp.dot(projb.astype(jnp.float32), local_columns), ("state", "rank"))
        mass = total / states_all
        raw_part = lax.dot_general(
            trans_left, projb, (((1,), (1,)), ((), ())), preferred_element_type=jnp.float32
        )
        raw = lax.psum(raw_part, "rank")
        beta = (raw / mass[None, :]).astype(jnp.bfloat16)
        weighted_list.insert(0, weighted)
        proj_list.insert(0, projb)
    weighted_all = jnp.concatenate(weighted_list, axis=1)
    proj_all = jnp.concatenate(proj_list, axis=0)
    count = steps * batch
    grad_left = (
        jnp.dot(forward_marg, proj_all, preferred_element_type=jnp.float32) / count
    ).astype(jnp.bfloat16)
    grad_right = (
        jnp.dot(weighted_all, fwd_proj, preferred_element_type=jnp.float32) / count
    ).astype(jnp.bfloat16)
    return (beta, grad_left, grad_right)


def solution(mesh):
    placed = (
        P(),
        P(),
        P("state", None),
        P("state"),
        P("state", None),
        P("state", None),
        P("state", "rank"),
        P("state", "rank"),
    )
    return jax.shard_map(
        on_device,
        mesh=mesh,
        in_specs=placed,
        out_specs=(P("state", None), P("state", "rank"), P("state", "rank")),
        check_vma=False,
    )
```

profile of v0, /device:TPU:1, one launch (start us, length us, event | category | flops | bytes accessed | tf_op | source)
XLA Modules:
  0.0 361.3 jit_solution(5714153270374027085)
XLA Ops:
  10.4 2.7 gather_fusion.2
  16.2 3.0 fusion.39
  19.2 34.0 %all-reduce.15 = bf16[128,512]{1,0:T(8,128)(2,1)S(1)} all-reduce(f32[128,512]{1,0:T(8,128)S(1)} %fusion.39), channel_id=1, replica_groups=mesh['state'=8,'rank'=4] {'state'}, use_global_device_ids=true, to_apply=%region_0.2 | all-reduce | flops 65536 | bytes 393216 | tf_op jit(solution)/shard_map/psum | solution.py:29
  53.2 5.0 %convolution_bitcast_fusion.2 = f32[4096,128]{0,1:T(8,128)} fusion(bf16[128,512]{1,0:T(8,128)(2,1)S(1)} %all-reduce.15, bf16[4096,512]{1,0:T(8,128)(2,1)} %param.16), kind=kOutput, calls=%fused_computation.9 | convolution fusion | flops 536870912 | bytes 6422528 | tf_op jit(solution)/shard_map/dot_general | solution.py:32
  58.3 2.7 gather_fusion.1
  61.0 2.8 convert_reduce_fusion
  63.9 45.1 %psum.72 = f32[128]{0:T(128)S(1)} all-reduce(f32[128]{0:T(128)S(1)} %convolution_bitcast_fusion.5), channel_id=1, replica_groups=mesh['state'=8,'rank'=4] {'state','rank'}, use_global_device_ids=true, to_apply=%region_3.5 | all-reduce | flops 128 | bytes 1024 | tf_op jit(solution)/shard_map/psum | solution.py:30
  109.1 6.4 %all-reduce.8.cloned.1.call-done = f32[4096,128]{0,1:T(8,128)} async-done(((f32[4096,128]{0,1:T(8,128)}), f32[4096,128]{0,1:T(8,128)}) %all-reduce.8.cloned.1.call-update) | async-done | bytes 2097168 | tf_op jit(solution)/shard_map/psum | solution.py:35
  115.5 2.6 fusion.11
  120.6 33.3 %all-reduce.16 = bf16[128,512]{1,0:T(8,128)(2,1)S(1)} all-reduce(f32[128,512]{1,0:T(8,128)} %fusion.40), channel_id=1, replica_groups=mesh['state'=8,'rank'=4] {'state'}, use_global_device_ids=true, to_apply=%region_4.6 | all-reduce | flops 65536 | bytes 393216 | tf_op jit(solution)/shard_map/psum | solution.py:29
  153.9 5.0 %convolution_bitcast_fusion.1 = f32[4096,128]{0,1:T(8,128)} fusion(bf16[128,512]{1,0:T(8,128)(2,1)S(1)} %all-reduce.16, bf16[4096,512]{1,0:T(8,128)(2,1)} %param.16), kind=kOutput, calls=%fused_computation.8 | convolution fusion | flops 536870912 | bytes 6422528 | tf_op jit(solution)/shard_map/dot_general | solution.py:32
  158.9 4.9 %fusion.42 = f32[384,512]{1,0:T(8,128)} fusion(bf16[4096,384]{1,0:T(8,128)(2,1)S(1)} %copy-done, bf16[4096,512]{1,0:T(8,128)(2,1)} %param.16), kind=kOutput, calls=%fused_computation.73 | convolution fusion | flops 1610612736 | bytes 8126464 | tf_op jit(solution)/shard_map/dot_general | solution.py:14
  163.9 2.7 gather_fusion
  166.7 45.1 %psum.75 = f32[128]{0:T(128)S(1)} all-reduce(f32[128]{0:T(128)S(1)} %convolution_bitcast_fusion.4), channel_id=1, replica_groups=mesh['state'=8,'rank'=4] {'state','rank'}, use_global_device_ids=true, to_apply=%region_6.8 | all-reduce | flops 128 | bytes 1024 | tf_op jit(solution)/shard_map/psum | solution.py:30
  211.8 3.7 %all-reduce.10.cloned.1.call-done = f32[4096,128]{0,1:T(8,128)} async-done(((f32[4096,128]{0,1:T(8,128)}), f32[4096,128]{0,1:T(8,128)}) %all-reduce.10.cloned.1.call-update) | async-done | bytes 2097168 | tf_op jit(solution)/shard_map/psum | solution.py:35
  215.5 2.6 fusion.10
  220.6 34.8 %all-reduce.17 = bf16[128,512]{1,0:T(8,128)(2,1)S(1)} all-reduce(f32[128,512]{1,0:T(8,128)} %fusion.41), channel_id=1, replica_groups=mesh['state'=8,'rank'=4] {'state'}, use_global_device_ids=true, to_apply=%region_7.9 | all-reduce | flops 65536 | bytes 393216 | tf_op jit(solution)/shard_map/psum | solution.py:29
  255.4 5.0 %convolution_bitcast_fusion = f32[4096,128]{0,1:T(8,128)} fusion(bf16[128,512]{1,0:T(8,128)(2,1)S(1)} %all-reduce.17, bf16[4096,512]{1,0:T(8,128)(2,1)} %param.16), kind=kOutput, calls=%fused_computation.7 | convolution fusion | flops 536870912 | bytes 6422528 | tf_op jit(solution)/shard_map/dot_general | solution.py:32
  260.4 4.4 %fusion = bf16[4096,512]{0,1:T(8,128)(2,1)} fusion(bf16[4096,384]{1,0:T(8,128)(2,1)S(1)} %copy-done, bf16[128,512]{1,0:T(8,128)(2,1)S(1)} %all-reduce.15, bf16[128,512]{1,0:T(8,128)(2,1)S(1)} %all-reduce.16, bf16[128,512]{1,0:T(8,128)(2,1)S(1)} %all-reduce.17), kind=kOutput, calls=%fused_computation.6 | convolution fusion | flops 1615986688 | bytes 7733248 | tf_op jit(solution)/shard_map/dot_general | solution.py:43
  264.8 6.4 %copy.13 = bf16[4096,512]{1,0:T(8,128)(2,1)} copy(bf16[4096,512]{0,1:T(8,128)(2,1)} %fusion) | data formatting | bytes 8388608
  271.3 45.1 %psum.78 = f32[128]{0:T(128)S(1)} all-reduce(f32[128]{0:T(128)S(1)} %convolution_bitcast_fusion.3), channel_id=1, replica_groups=mesh['state'=8,'rank'=4] {'state','rank'}, use_global_device_ids=true, to_apply=%region_9.11 | all-reduce | flops 128 | bytes 1024 | tf_op jit(solution)/shard_map/psum | solution.py:30
  316.5 6.5 %multiply_convert_fusion = bf16[4096,512]{1,0:T(8,128)(2,1)} fusion(bf16[4096,128]{0,1:T(8,128)(2,1)} %copy-done.3, bf16[4096,128]{0,1:T(8,128)(2,1)} %copy-done.4, bf16[4096,128]{0,1:T(8,128)(2,1)} %copy-done.5, f32[384,512]{1,0:T(8,128)} %all-reduce.14.cloned.1.call-done), kind=kOutput, calls=%fused_computation.3 | convolution fusion | flops 1624637440 | bytes 8126464 | tf_op jit(solution)/shard_map/dot_general | solution.py:46
  323.0 26.8 %all-reduce.12.cloned.1.call-done = f32[4096,128]{0,1:T(8,128)} async-done(((f32[4096,128]{0,1:T(8,128)}), f32[4096,128]{0,1:T(8,128)}) %all-reduce.12.cloned.1.call-update) | async-done | bytes 2097168 | tf_op jit(solution)/shard_map/psum | solution.py:35
  349.7 2.8 divide_convert_fusion
  (38 shorter events, 14.0 us)
Async XLA Ops:
  7.2 151.8 %copy-start = (bf16[4096,384]{1,0:T(8,128)(2,1)S(1)}, bf16[4096,384]{1,0:T(8,128)(2,1)}, u32[]{:S(2)}) copy-start(bf16[4096,384]{1,0:T(8,128)(2,1)} %param.15) | copy-start | bytes 9437188
  7.2 108.3 %all-reduce.8.cloned.1.call-start = ((), (), s32[]{:S(2)}) async-start(), calls=%async_computation | async-start | bytes 4194304 | tf_op jit(solution)/shard_map/psum | solution.py:35
  15.3 1.0 copy-start.3
  58.2 57.3 %copy-start.6 = (f32[4096]{0:T(1024)S(1)}, f32[4096]{0:T(1024)}, u32[]{:S(2)}) copy-start(f32[4096]{0:T(1024)} %param.13) | copy-start | bytes 49156
  58.2 157.3 %all-reduce.10.cloned.1.call-start = ((), (), s32[]{:S(2)}) async-start(), calls=%async_computation.1 | async-start | bytes 4194304 | tf_op jit(solution)/shard_map/psum | solution.py:35
  115.5 3.6 %copy-start.1 = (bf16[4096,512]{1,0:T(8,128)(2,1)S(1)}, bf16[4096,512]{1,0:T(8,128)(2,1)}, u32[]{:S(2)}) copy-start(bf16[4096,512]{1,0:T(8,128)(2,1)} %param.17) | copy-start | bytes 12582916
  118.2 1.0 copy-start.4
  158.9 157.6 %all-reduce.14.cloned.1.call-start = ((), (), s32[]{:S(2)}) async-start(), calls=%async_computation.3 | async-start | bytes 1572864 | tf_op jit(solution)/shard_map/psum | solution.py:17
  163.8 185.9 %all-reduce.12.cloned.1.call-start = ((), (), s32[]{:S(2)}) async-start(), calls=%async_computation.2 | async-start | bytes 4194304 | tf_op jit(solution)/shard_map/psum | solution.py:35
  215.5 3.7 %copy-start.2 = (bf16[4096,512]{1,0:T(8,128)(2,1)S(1)}, bf16[4096,512]{1,0:T(8,128)(2,1)}, u32[]{:S(2)}) copy-start(bf16[4096,512]{1,0:T(8,128)(2,1)} %param.17) | copy-start | bytes 12582916
  218.2 1.0 copy-start.5
Sparse Core Ops, SparseCore 0:
  58.4 57.1 all-reduce.7
  159.0 56.4 all-reduce.9
  219.0 76.2 all-reduce.13
  297.6 52.1 all-reduce.11
where the time goes:
time: 363 us; the launch traced here: 361 us
  blocking collectives  237 us (65%)
  matrix products  44.3 us (12%)
  waiting for transfers between devices  37 us (10%)
  local copies, waits for them, and re-layouts  22 us (6%)
  between operations  13.9 us (4%)
  other arithmetic  6.5 us (2%)
    psum x3, blocking collectives, on_device(): lax.psum(jnp.dot(projb.astype(jnp.float32), local_columns), ('state', 'ra...  135 us
    psum x3, blocking collectives, on_device(): projb = lax.psum(proj_part, 'state').astype(jnp.bfloat16)  102 us
    psum x3, waiting for transfers between devices, on_device(): raw = lax.psum(raw_part, 'rank')  36.9 us
    dot_general x3, matrix products, on_device(): lax.dot_general(trans_left, projb, (((1,), (1,)), ((), ())), preferred_el...  14.9 us
    unnamed x17, local copies, waits for them, and re-layouts  13.9 us
    gather x3, local copies, waits for them, and re-layouts, on_device(): words = jnp.take(word_emb, token_ids[step], axis=0)  8.1 us
    dot_general x3, matrix products, on_device(): logits = jnp.dot(state_emb, words.T, preferred_element_type=jnp.float32)  7.39 us
  transfers between devices with their start and end apart: 4, of which 3 were waited for; matrix products, arithmetic and copies ran while one was open for 11% of the time, Pallas kernels for 0%

commit v1 on v0

v1 whole, which is shorter than its diff:
```python
import jax
import jax.numpy as jnp
from jax import lax
from jax.sharding import PartitionSpec as P


def send_by(value, axis, offset):
    count = lax.axis_size(axis)
    return lax.ppermute(value, axis, [(i, (i + offset) % count) for i in range(count)])


def send_xor(value, axis, bit):
    count = lax.axis_size(axis)
    return lax.ppermute(value, axis, [(i, i ^ bit) for i in range(count)])


def sum_small(value, axis):
    bit = 1
    while bit < lax.axis_size(axis):
        value = value + send_xor(value, axis, bit)
        bit *= 2
    return value


def sum_over_state(part, scale):
    count = lax.axis_size("state")
    me = lax.axis_index("state")
    rows, columns = part.shape
    pieces = part.astype(jnp.bfloat16).reshape(count, rows // count, columns)

    def piece(index):
        return lax.dynamic_index_in_dim(pieces, index % count, 0, keepdims=False)

    total = lax.dynamic_index_in_dim(
        part.reshape(count, rows // count, columns), me, 0, keepdims=False
    )
    for offset in range(1, count):
        got = send_by(piece(me + offset), "state", offset)
        total = total + got.astype(jnp.float32)
    mine = (total * scale).astype(jnp.bfloat16)
    held = [mine] + [send_by(mine, "state", offset) for offset in range(1, count)]
    stacked = jnp.stack(held[::-1])
    ordered = jnp.roll(stacked, me + 1, axis=0)
    return ordered.reshape(rows, columns)


def sum_over_rank(raw_part, mass_part):
    count = lax.axis_size("rank")
    me = lax.axis_index("rank")
    half = raw_part.shape[0] // 2
    low = me % 2
    own = lax.dynamic_slice_in_dim(raw_part, low * half, half, 0)
    other = lax.dynamic_slice_in_dim(raw_part, (1 - low) * half, half, 0)
    total = own + send_xor(other.astype(jnp.bfloat16), "rank", 1).astype(jnp.float32)
    bit = 2
    while bit < count:
        rounded = total.astype(jnp.bfloat16)
        got = send_xor(rounded, "rank", bit)
        total = rounded.astype(jnp.float32) + got.astype(jnp.float32)
        bit *= 2
    mass = sum_small(mass_part, "rank")
    return total, mass


def both_halves(value):
    low = lax.axis_index("rank") % 2
    got = send_xor(value, "rank", 1)
    first = jnp.where(low == 0, value, got)
    second = jnp.where(low == 0, got, value)
    return jnp.concatenate([first, second], axis=0)


def on_device(
    token_ids, word_emb, state_emb, log_norm, beta_last, forward_marg, trans_left, trans_right
):
    states_all = lax.axis_size("state") * state_emb.shape[0]
    steps, batch = token_ids.shape
    column_sums = sum_small(jnp.sum(trans_left, axis=0, dtype=jnp.float32), "state")
    words_all = jnp.take(word_emb, token_ids.reshape(-1), axis=0)
    logits = jnp.dot(state_emb, words_all.T, preferred_element_type=jnp.float32)
    emit_all = jnp.exp(logits - log_norm[:, None])
    beta = beta_last
    weighted_list = []
    proj_list = []
    fwd_proj = None
    for step in reversed(range(steps)):
        emit = emit_all[:, step * batch : (step + 1) * batch]
        weighted = (emit * beta.astype(jnp.float32)).astype(jnp.bfloat16)
        proj_part = lax.dot_general(
            weighted, trans_right, (((0,), (0,)), ((), ())), preferred_element_type=jnp.float32
        )
        projb = sum_over_state(proj_part, 1.0)
        mass_part = jnp.dot(projb.astype(jnp.float32), column_sums)
        raw_part = lax.dot_general(
            trans_left, projb, (((1,), (1,)), ((), ())), preferred_element_type=jnp.float32
        )
        raw_half, total = sum_over_rank(raw_part, mass_part)
        mass = total / states_all
        beta = both_halves((raw_half / mass[None, :]).astype(jnp.bfloat16))
        if fwd_proj is None:
            fwd_part = lax.dot_general(
                forward_marg,
                trans_left,
                (((0,), (0,)), ((), ())),
                preferred_element_type=jnp.float32,
            )
            fwd_proj = sum_over_state(fwd_part, 1.0 / states_all)
        weighted_list.insert(0, weighted)
        proj_list.insert(0, projb)
    weighted_all = jnp.concatenate(weighted_list, axis=1)
    proj_all = jnp.concatenate(proj_list, axis=0)
    count = steps * batch
    grad_left = (
        jnp.dot(forward_marg, proj_all, preferred_element_type=jnp.float32) / count
    ).astype(jnp.bfloat16)
    grad_right = (
        jnp.dot(weighted_all, fwd_proj, preferred_element_type=jnp.float32) / count
    ).astype(jnp.bfloat16)
    return (beta, grad_left, grad_right)


def solution(mesh):
    placed = (
        P(),
        P(),
        P("state", None),
        P("state"),
        P("state", None),
        P("state", None),
        P("state", "rank"),
        P("state", "rank"),
    )
    return jax.shard_map(
        on_device,
        mesh=mesh,
        in_specs=placed,
        out_specs=(P("state", None), P("state", "rank"), P("state", "rank")),
        check_vma=False,
    )
```

time: 363 us -> 255 us (0.70)
  blocking collectives: 237 us -> 0 us
  starting transfers between devices: 0.16 us -> 119 us
  waiting for transfers between devices: 37 us -> 71.1 us
  matrix products: 44.3 us -> 22.6 us
  between operations: 13.9 us -> 1.24 us
  other arithmetic: 6.5 us -> 17.9 us
    psum x6 -> x0, blocking collectives: 237 us -> none  [the longest x3 135 us: on_device(): lax.psum(jnp.dot(projb.astype(jnp.float32), local_columns), ('state', 'ra...]
    ppermute x0 -> x74, starting transfers between devices: none -> 119 us  [the longest x56 79.5 us: send_by(): lax.ppermute(value, axis, [(i, (i + offset) % count) for i in range(count)])]
    ppermute x0 -> x74, waiting for transfers between devices: none -> 71.1 us  [the longest x18 39.2 us: send_xor(): return lax.ppermute(value, axis, [(i, i ^ bit) for i in range(count)])]
    psum x4 -> x0, waiting for transfers between devices: 36.9 us -> none  [the longest x3 36.9 us: on_device(): raw = lax.psum(raw_part, 'rank')]
    dot_general x3, matrix products: 14.9 us -> 6.58 us  [on_device(): lax.dot_general(trans_left, projb, (((1,), (1,)), ((), ())), preferred_el...]
    convert_element_type x1 -> x13, other arithmetic: 2.8 us -> 9.67 us  [the longest x3 3.9 us: on_device(): weighted = (emit * beta.astype(jnp.float32)).astype(jnp.bfloat16)]
    dot_general x6 -> x4, matrix products: 7.77 us -> 2.72 us  [the longest x1 2.34 us: on_device(): logits = jnp.dot(state_emb, words_all.T, preferred_element_type=jnp.float32)]
    gather x3 -> x1, local copies, waits for them, and re-layouts: 8.1 us -> 3.22 us  [on_device(): words_all = jnp.take(word_emb, token_ids.reshape(-1), axis=0)]
  transfers between devices with their start and end apart: 4 -> 74, of which waited for: 3 -> 33; matrix products, arithmetic and copies ran while one was open for 11% -> 11% of each run, Pallas kernels for 0% -> 0%
where the time goes in v1:
time: 255 us; the launch traced here: 254 us
  starting transfers between devices  119 us (47%)
  waiting for transfers between devices  71.1 us (28%)
  matrix products  22.6 us (9%)
  local copies, waits for them, and re-layouts  21.9 us (9%)
  other arithmetic  17.9 us (7%)
    ppermute x56, starting transfers between devices, send_by(): lax.ppermute(value, axis, [(i, (i + offset) % count) for i in range(count)])  79.5 us
    ppermute x18, starting transfers between devices, send_xor(): return lax.ppermute(value, axis, [(i, i ^ bit) for i in range(count)])  39.7 us
    ppermute x18, waiting for transfers between devices, send_xor(): return lax.ppermute(value, axis, [(i, i ^ bit) for i in range(count)])  39.2 us
    ppermute x56, waiting for transfers between devices, send_by(): lax.ppermute(value, axis, [(i, (i + offset) % count) for i in range(count)])  31.9 us
    unnamed x59, local copies, waits for them, and re-layouts  16.9 us
    dot_general x3, matrix products, on_device(): lax.dot_general(trans_left, projb, (((1,), (1,)), ((), ())), preferred_el...  6.58 us
  transfers between devices with their start and end apart: 74, of which 33 were waited for; matrix products, arithmetic and copies ran while one was open for 11% of the time, Pallas kernels for 0%

profile of v1, /device:TPU:1, one launch (start us, length us, event | category | flops | bytes accessed | tf_op | source)
XLA Modules:
  0.0 254.0 jit_solution(10596378084153648859)
XLA Ops:
  4.6 3.2 %gather_fusion = bf16[384,128]{1,0:T(8,128)(2,1)S(1)} fusion(bf16[10000,128]{1,0:T(8,128)(2,1)} %param.11, s32[1024]{0:T(1024)S(1)} %pad_clamp_fusion), kind=kCustom, calls=%fused_computation | custom fusion | bytes 198144 | tf_op jit(solution)/shard_map/jit(_take)/gather | solution.py:79
  10.4 4.2 %copy-done.3 = bf16[4096,512]{1,0:T(8,128)(2,1)S(1)} copy-done((bf16[4096,512]{1,0:T(8,128)(2,1)S(1)}, bf16[4096,512]{1,0:T(8,128)(2,1)}, u32[]{:S(2)}) %copy-start.3) | copy-done | bytes 4194328
  29.2 4.0 %collective-permute-start.7 = (bf16[16,512]{1,0:T(8,128)(2,1)S(1)}, bf16[16,512]{1,0:T(8,128)(2,1)S(1)}, u32[]{:S(2)}, u32[]{:S(2)}) collective-permute-start(bf16[16,512]{1,0:T(8,128)(2,1)S(1)} %fusion.54), channel_id=1, source_target_pairs={{0,28},{4,0},{8,4},{12,8},{16,12},{20,16},{24,20},{28,24},{1,29},{... | collective-permute-start | bytes 49160 | tf_op jit(solution)/shard_map/ppermute | solution.py:9
  42.5 3.7 %fusion.63 = f32[128,4096]{1,0:T(8,128)S(1)} fusion(bf16[128,512]{1,0:T(8,128)(2,1)S(1)} %bitcast.269, bf16[4096,512]{1,0:T(8,128)(2,1)} %param.16), kind=kOutput, calls=%fused_computation.176 | convolution fusion | flops 536870912 | bytes 6422528 | tf_op jit(solution)/shard_map/dot_general | solution.py:94
  48.3 5.8 %collective-permute-start.14 = (bf16[2048,128]{0,1:T(8,128)(2,1)}, bf16[2048,128]{0,1:T(8,128)(2,1)}, u32[]{:S(2)}, u32[]{:S(2)}) collective-permute-start(bf16[2048,128]{0,1:T(8,128)(2,1)} %fusion.12), channel_id=1, source_target_pairs={{0,1},{1,0},{2,3},{3,2},{4,5},{5,4},{6,7},{7,6},{8,9},{9,8},{10,11... | collective-permute-start | bytes 1572872 | tf_op jit(solution)/shard_map/ppermute | solution.py:14
  58.8 2.8 %convert_reduce_fusion = f32[512]{0:T(512)S(1)} fusion(bf16[4096,512]{1,0:T(8,128)(2,1)} %param.16), kind=kLoop, calls=%fused_computation.3 | loop fusion | flops 4193792 | bytes 4196352 | tf_op jit(solution)/shard_map/reduce_sum | solution.py:78
  70.6 3.5 %collective-permute-start.19 = (f32[128]{0:T(128)S(1)}, f32[128]{0:T(128)S(1)}, u32[]{:S(2)}, u32[]{:S(2)}) collective-permute-start(f32[128]{0:T(128)S(1)} %convolution_bitcast_fusion.2), channel_id=1, source_target_pairs={{0,1},{1,0},{2,3},{3,2},{4,5},{5,4},{6,7},{7,6},{8,9},{9,8},{10,11... | collective-permute-start | bytes 1544 | tf_op jit(solution)/shard_map/ppermute | solution.py:14
  90.6 3.2 %collective-permute-done.62 = bf16[48,512]{1,0:T(8,128)(2,1)S(1)} collective-permute-done((bf16[48,512]{1,0:T(8,128)(2,1)S(1)}, bf16[48,512]{1,0:T(8,128)(2,1)S(1)}, u32[]{:S(2)}, u32[]{:S(2)}) %collective-permute-start.62) | collective-permute-done | bytes 49184 | tf_op jit(solution)/shard_map/ppermute | solution.py:9
  97.9 2.8 %collective-permute-start.67 = (bf16[48,512]{1,0:T(8,128)(2,1)S(1)}, bf16[48,512]{1,0:T(8,128)(2,1)S(1)}, u32[]{:S(2)}, u32[]{:S(2)}) collective-permute-start(bf16[48,512]{1,0:T(8,128)(2,1)S(1)} %fusion.30), channel_id=1, source_target_pairs={{0,28},{4,0},{8,4},{12,8},{16,12},{20,16},{24,20},{28,24},{1,29},{... | collective-permute-start | bytes 147464 | tf_op jit(solution)/shard_map/ppermute | solution.py:9
  106.9 3.7 %collective-permute-start.25 = (bf16[16,512]{1,0:T(8,128)(2,1)S(1)}, bf16[16,512]{1,0:T(8,128)(2,1)S(1)}, u32[]{:S(2)}, u32[]{:S(2)}) collective-permute-start(bf16[16,512]{1,0:T(8,128)(2,1)S(1)} %get-tuple-element.31), channel_id=1, source_target_pairs={{0,16},{4,20},{8,24},{12,28},{16,0},{20,4},{24,8},{28,12},{1,17},{... | collective-permute-start | bytes 49160 | tf_op jit(solution)/shard_map/ppermute | solution.py:9
  119.0 4.2 %collective-permute-start.29 = (bf16[16,512]{1,0:T(8,128)(2,1)S(1)}, bf16[16,512]{1,0:T(8,128)(2,1)S(1)}, u32[]{:S(2)}, u32[]{:S(2)}) collective-permute-start(bf16[16,512]{1,0:T(8,128)(2,1)S(1)} %fusion.47), channel_id=1, source_target_pairs={{0,28},{4,0},{8,4},{12,8},{16,12},{20,16},{24,20},{28,24},{1,29},{... | collective-permute-start | bytes 49160 | tf_op jit(solution)/shard_map/ppermute | solution.py:9
  127.1 3.0 %collective-permute-start.31 = (bf16[16,512]{1,0:T(8,128)(2,1)S(1)}, bf16[16,512]{1,0:T(8,128)(2,1)S(1)}, u32[]{:S(2)}, u32[]{:S(2)}) collective-permute-start(bf16[16,512]{1,0:T(8,128)(2,1)S(1)} %fusion.47), channel_id=1, source_target_pairs={{0,20},{4,24},{8,28},{12,0},{16,4},{20,8},{24,12},{28,16},{1,21},{... | collective-permute-start | bytes 49160 | tf_op jit(solution)/shard_map/ppermute | solution.py:9
  130.9 3.5 %collective-permute-start.32 = (bf16[16,512]{1,0:T(8,128)(2,1)S(1)}, bf16[16,512]{1,0:T(8,128)(2,1)S(1)}, u32[]{:S(2)}, u32[]{:S(2)}) collective-permute-start(bf16[16,512]{1,0:T(8,128)(2,1)S(1)} %fusion.47), channel_id=1, source_target_pairs={{0,16},{4,20},{8,24},{12,28},{16,0},{20,4},{24,8},{28,12},{1,17},{... | collective-permute-start | bytes 49160 | tf_op jit(solution)/shard_map/ppermute | solution.py:9
  135.6 3.3 %collective-permute-start.33 = (bf16[16,512]{1,0:T(8,128)(2,1)S(1)}, bf16[16,512]{1,0:T(8,128)(2,1)S(1)}, u32[]{:S(2)}, u32[]{:S(2)}) collective-permute-start(bf16[16,512]{1,0:T(8,128)(2,1)S(1)} %fusion.47), channel_id=1, source_target_pairs={{0,12},{4,16},{8,20},{12,24},{16,28},{20,0},{24,4},{28,8},{1,13},{... | collective-permute-start | bytes 49160 | tf_op jit(solution)/shard_map/ppermute | solution.py:9
  144.4 3.0 %collective-permute-start.35 = (bf16[16,512]{1,0:T(8,128)(2,1)S(1)}, bf16[16,512]{1,0:T(8,128)(2,1)S(1)}, u32[]{:S(2)}, u32[]{:S(2)}) collective-permute-start(bf16[16,512]{1,0:T(8,128)(2,1)S(1)} %fusion.47), channel_id=1, source_target_pairs={{0,4},{4,8},{8,12},{12,16},{16,20},{20,24},{24,28},{28,0},{1,5},{5... | collective-permute-start | bytes 49160 | tf_op jit(solution)/shard_map/ppermute | solution.py:9
  151.3 13.7 %collective-permute-start.36 = (bf16[2048,128]{0,1:T(8,128)(2,1)S(1)}, bf16[2048,128]{0,1:T(8,128)(2,1)S(1)}, u32[]{:S(2)}, u32[]{:S(2)}) collective-permute-start(bf16[2048,128]{0,1:T(8,128)(2,1)S(1)} %fusion.13), channel_id=1, source_target_pairs={{0,1},{1,0},{2,3},{3,2},{4,5},{5,4},{6,7},{7,6},{8,9},{9,8},{10,11... | collective-permute-start | bytes 1572872 | tf_op jit(solution)/shard_map/ppermute | solution.py:14
  168.3 11.6 %collective-permute-done.39 = f32[128]{0:T(128)S(1)} collective-permute-done((f32[128]{0:T(128)S(1)}, f32[128]{0:T(128)S(1)}, u32[]{:S(2)}, u32[]{:S(2)}) %collective-permute-start.39) | collective-permute-done | bytes 544 | tf_op jit(solution)/shard_map/ppermute | solution.py:14
  186.5 3.8 %collective-permute-start.44 = (bf16[16,512]{1,0:T(8,128)(2,1)S(1)}, bf16[16,512]{1,0:T(8,128)(2,1)S(1)}, u32[]{:S(2)}, u32[]{:S(2)}) collective-permute-start(bf16[16,512]{1,0:T(8,128)(2,1)S(1)} %get-tuple-element.24), channel_id=1, source_target_pairs={{0,16},{4,20},{8,24},{12,28},{16,0},{20,4},{24,8},{28,12},{1,17},{... | collective-permute-start | bytes 49160 | tf_op jit(solution)/shard_map/ppermute | solution.py:9
  195.9 3.3 %collective-permute-start.48 = (bf16[16,512]{1,0:T(8,128)(2,1)S(1)}, bf16[16,512]{1,0:T(8,128)(2,1)S(1)}, u32[]{:S(2)}, u32[]{:S(2)}) collective-permute-start(bf16[16,512]{1,0:T(8,128)(2,1)S(1)} %fusion.40), channel_id=1, source_target_pairs={{0,28},{4,0},{8,4},{12,8},{16,12},{20,16},{24,20},{28,24},{1,29},{... | collective-permute-start | bytes 49160 | tf_op jit(solution)/shard_map/ppermute | solution.py:9
  211.6 5.9 %collective-permute-start.55 = (bf16[2048,128]{0,1:T(8,128)(2,1)S(1)}, bf16[2048,128]{0,1:T(8,128)(2,1)S(1)}, u32[]{:S(2)}, u32[]{:S(2)}) collective-permute-start(bf16[2048,128]{0,1:T(8,128)(2,1)S(1)} %fusion.14), channel_id=1, source_target_pairs={{0,1},{1,0},{2,3},{3,2},{4,5},{5,4},{6,7},{7,6},{8,9},{9,8},{10,11... | collective-permute-start | bytes 1572872 | tf_op jit(solution)/shard_map/ppermute | solution.py:14
  220.8 11.6 %collective-permute-done.58 = f32[128]{0:T(128)S(1)} collective-permute-done((f32[128]{0:T(128)S(1)}, f32[128]{0:T(128)S(1)}, u32[]{:S(2)}, u32[]{:S(2)}) %collective-permute-start.58) | collective-permute-done | bytes 544 | tf_op jit(solution)/shard_map/ppermute | solution.py:14
  234.6 3.9 %multiply_convert_fusion = bf16[4096,512]{1,0:T(8,128)(2,1)} fusion(bf16[384,512]{1,0:T(8,128)(2,1)S(1)} %bitcast.281, bf16[4096,128]{0,1:T(8,128)(2,1)S(1)} %copy-done.9, bf16[4096,128]{0,1:T(8,128)(2,1)S(1)} %fusion.7, bf16[4096,128]{0,1:T(8,128)(2,1)S(1)} %fusion.8), kind=kOutput, calls=%fused_computation.1 | convolution fusion | flops 1624244224 | bytes 7733248 | tf_op jit(solution)/shard_map/dot_general | solution.py:117
  238.5 4.4 %fusion = bf16[4096,512]{0,1:T(8,128)(2,1)} fusion(bf16[4096,384]{1,0:T(8,128)(2,1)S(1)} %copy-done, bf16[128,512]{1,0:T(8,128)(2,1)S(1)} %bitcast.271, bf16[128,512]{1,0:T(8,128)(2,1)S(1)} %bitcast.274, bf16[128,512]{1,0:T(8,128)(2,1)S(1)} %bitcast.277), kind=kOutput, calls=%fused_computation.5 | convolution fusion | flops 1615986688 | bytes 7733248 | tf_op jit(solution)/shard_map/dot_general | solution.py:114
  243.0 6.4 %copy.13 = bf16[4096,512]{1,0:T(8,128)(2,1)} copy(bf16[4096,512]{0,1:T(8,128)(2,1)} %fusion) | data formatting | bytes 8388608
  (242 shorter events, 134.2 us)
Async XLA Ops:
  15.6 9.0 %collective-permute-start = (bf16[16,512]{1,0:T(8,128)(2,1)S(1)}, bf16[16,512]{1,0:T(8,128)(2,1)S(1)}, u32[]{:S(2)}, u32[]{:S(2)}) collective-permute-start(bf16[16,512]{1,0:T(8,128)(2,1)S(1)} %get-tuple-element.34), channel_id=1, source_target_pairs={{0,4},{4,8},{8,12},{12,16},{16,20},{20,24},{24,28},{28,0},{1,5},{5... | collective-permute-start | bytes 49160 | tf_op jit(solution)/shard_map/ppermute | solution.py:9
  17.7 7.9 %collective-permute-start.1 = (bf16[16,512]{1,0:T(8,128)(2,1)S(1)}, bf16[16,512]{1,0:T(8,128)(2,1)S(1)}, u32[]{:S(2)}, u32[]{:S(2)}) collective-permute-start(bf16[16,512]{1,0:T(8,128)(2,1)S(1)} %get-tuple-element.40), channel_id=1, source_target_pairs={{0,8},{4,12},{8,16},{12,20},{16,24},{20,28},{24,0},{28,4},{1,9},{5... | collective-permute-start | bytes 49160 | tf_op jit(solution)/shard_map/ppermute | solution.py:9
  19.0 7.8 %collective-permute-start.2 = (bf16[16,512]{1,0:T(8,128)(2,1)S(1)}, bf16[16,512]{1,0:T(8,128)(2,1)S(1)}, u32[]{:S(2)}, u32[]{:S(2)}) collective-permute-start(bf16[16,512]{1,0:T(8,128)(2,1)S(1)} %get-tuple-element.39), channel_id=1, source_target_pairs={{0,12},{4,16},{8,20},{12,24},{16,28},{20,0},{24,4},{28,8},{1,13},{... | collective-permute-start | bytes 49160 | tf_op jit(solution)/shard_map/ppermute | solution.py:9
  48.3 7.7 %collective-permute-start.14 = (bf16[2048,128]{0,1:T(8,128)(2,1)}, bf16[2048,128]{0,1:T(8,128)(2,1)}, u32[]{:S(2)}, u32[]{:S(2)}) collective-permute-start(bf16[2048,128]{0,1:T(8,128)(2,1)} %fusion.12), channel_id=1, source_target_pairs={{0,1},{1,0},{2,3},{3,2},{4,5},{5,4},{6,7},{7,6},{8,9},{9,8},{10,11... | collective-permute-start | bytes 1572872 | tf_op jit(solution)/shard_map/ppermute | solution.py:14
  57.5 19.9 %collective-permute-start.15 = (bf16[2048,128]{0,1:T(8,128)(2,1)S(1)}, bf16[2048,128]{0,1:T(8,128)(2,1)S(1)}, u32[]{:S(2)}, u32[]{:S(2)}) collective-permute-start(bf16[2048,128]{0,1:T(8,128)(2,1)S(1)} %fusion.11), channel_id=1, source_target_pairs={{0,2},{1,3},{2,0},{3,1},{4,6},{5,7},{6,4},{7,5},{8,10},{9,11},{10,... | collective-permute-start | bytes 1572872 | tf_op jit(solution)/shard_map/ppermute | solution.py:14
  78.4 22.3 %collective-permute-start.21 = (bf16[2048,128]{0,1:T(8,128)(2,1)}, bf16[2048,128]{0,1:T(8,128)(2,1)}, u32[]{:S(2)}, u32[]{:S(2)}) collective-permute-start(bf16[2048,128]{0,1:T(8,128)(2,1)} %divide_convert_fusion.2), channel_id=1, source_target_pairs={{0,1},{1,0},{2,3},{3,2},{4,5},{5,4},{6,7},{7,6},{8,9},{9,8},{10,11... | collective-permute-start | bytes 1572872 | tf_op jit(solution)/shard_map/ppermute | solution.py:14
  83.5 10.3 %collective-permute-start.62 = (bf16[48,512]{1,0:T(8,128)(2,1)S(1)}, bf16[48,512]{1,0:T(8,128)(2,1)S(1)}, u32[]{:S(2)}, u32[]{:S(2)}) collective-permute-start(bf16[48,512]{1,0:T(8,128)(2,1)S(1)} %get-tuple-element.18), channel_id=1, source_target_pairs={{0,12},{4,16},{8,20},{12,24},{16,28},{20,0},{24,4},{28,8},{1,13},{... | collective-permute-start | bytes 147464 | tf_op jit(solution)/shard_map/ppermute | solution.py:9
  86.1 7.7 %collective-permute-start.63 = (bf16[48,512]{1,0:T(8,128)(2,1)}, bf16[48,512]{1,0:T(8,128)(2,1)}, u32[]{:S(2)}, u32[]{:S(2)}) collective-permute-start(bf16[48,512]{1,0:T(8,128)(2,1)} %get-tuple-element.17), channel_id=1, source_target_pairs={{0,16},{4,20},{8,24},{12,28},{16,0},{20,4},{24,8},{28,12},{1,17},{... | collective-permute-start | bytes 147464 | tf_op jit(solution)/shard_map/ppermute | solution.py:9
  97.9 8.2 %collective-permute-start.67 = (bf16[48,512]{1,0:T(8,128)(2,1)S(1)}, bf16[48,512]{1,0:T(8,128)(2,1)S(1)}, u32[]{:S(2)}, u32[]{:S(2)}) collective-permute-start(bf16[48,512]{1,0:T(8,128)(2,1)S(1)} %fusion.30), channel_id=1, source_target_pairs={{0,28},{4,0},{8,4},{12,8},{16,12},{20,16},{24,20},{28,24},{1,29},{... | collective-permute-start | bytes 147464 | tf_op jit(solution)/shard_map/ppermute | solution.py:9
  100.7 9.9 %collective-permute-start.68 = (bf16[48,512]{1,0:T(8,128)(2,1)S(1)}, bf16[48,512]{1,0:T(8,128)(2,1)S(1)}, u32[]{:S(2)}, u32[]{:S(2)}) collective-permute-start(bf16[48,512]{1,0:T(8,128)(2,1)S(1)} %fusion.30), channel_id=1, source_target_pairs={{0,24},{4,28},{8,0},{12,4},{16,8},{20,12},{24,16},{28,20},{1,25},{... | collective-permute-start | bytes 147464 | tf_op jit(solution)/shard_map/ppermute | solution.py:9
  105.0 7.8 %collective-permute-start.23 = (bf16[16,512]{1,0:T(8,128)(2,1)S(1)}, bf16[16,512]{1,0:T(8,128)(2,1)S(1)}, u32[]{:S(2)}, u32[]{:S(2)}) collective-permute-start(bf16[16,512]{1,0:T(8,128)(2,1)S(1)} %get-tuple-element.33), channel_id=1, source_target_pairs={{0,8},{4,12},{8,16},{12,20},{16,24},{20,28},{24,0},{28,4},{1,9},{5... | collective-permute-start | bytes 49160 | tf_op jit(solution)/shard_map/ppermute | solution.py:9
  106.2 7.7 %collective-permute-start.24 = (bf16[16,512]{1,0:T(8,128)(2,1)S(1)}, bf16[16,512]{1,0:T(8,128)(2,1)S(1)}, u32[]{:S(2)}, u32[]{:S(2)}) collective-permute-start(bf16[16,512]{1,0:T(8,128)(2,1)S(1)} %get-tuple-element.32), channel_id=1, source_target_pairs={{0,12},{4,16},{8,20},{12,24},{16,28},{20,0},{24,4},{28,8},{1,13},{... | collective-permute-start | bytes 49160 | tf_op jit(solution)/shard_map/ppermute | solution.py:9
  106.9 7.4 %collective-permute-start.25 = (bf16[16,512]{1,0:T(8,128)(2,1)S(1)}, bf16[16,512]{1,0:T(8,128)(2,1)S(1)}, u32[]{:S(2)}, u32[]{:S(2)}) collective-permute-start(bf16[16,512]{1,0:T(8,128)(2,1)S(1)} %get-tuple-element.31), channel_id=1, source_target_pairs={{0,16},{4,20},{8,24},{12,28},{16,0},{20,4},{24,8},{28,12},{1,17},{... | collective-permute-start | bytes 49160 | tf_op jit(solution)/shard_map/ppermute | solution.py:9
  114.3 50.7 %collective-permute-start.70 = (bf16[48,512]{1,0:T(8,128)(2,1)S(1)}, bf16[48,512]{1,0:T(8,128)(2,1)S(1)}, u32[]{:S(2)}, u32[]{:S(2)}) collective-permute-start(bf16[48,512]{1,0:T(8,128)(2,1)S(1)} %fusion.30), channel_id=1, source_target_pairs={{0,16},{4,20},{8,24},{12,28},{16,0},{20,4},{24,8},{28,12},{1,17},{... | collective-permute-start | bytes 147464 | tf_op jit(solution)/shard_map/ppermute | solution.py:9
  116.4 48.7 %collective-permute-start.71 = (bf16[48,512]{1,0:T(8,128)(2,1)S(1)}, bf16[48,512]{1,0:T(8,128)(2,1)S(1)}, u32[]{:S(2)}, u32[]{:S(2)}) collective-permute-start(bf16[48,512]{1,0:T(8,128)(2,1)S(1)} %fusion.30), channel_id=1, source_target_pairs={{0,12},{4,16},{8,20},{12,24},{16,28},{20,0},{24,4},{28,8},{1,13},{... | collective-permute-start | bytes 147464 | tf_op jit(solution)/shard_map/ppermute | solution.py:9
  117.5 49.5 %collective-permute-start.72 = (bf16[48,512]{1,0:T(8,128)(2,1)S(1)}, bf16[48,512]{1,0:T(8,128)(2,1)S(1)}, u32[]{:S(2)}, u32[]{:S(2)}) collective-permute-start(bf16[48,512]{1,0:T(8,128)(2,1)S(1)} %fusion.30), channel_id=1, source_target_pairs={{0,8},{4,12},{8,16},{12,20},{16,24},{20,28},{24,0},{28,4},{1,9},{5... | collective-permute-start | bytes 147464 | tf_op jit(solution)/shard_map/ppermute | solution.py:9
  118.9 49.4 %collective-permute-start.73 = (bf16[48,512]{1,0:T(8,128)(2,1)S(1)}, bf16[48,512]{1,0:T(8,128)(2,1)S(1)}, u32[]{:S(2)}, u32[]{:S(2)}) collective-permute-start(bf16[48,512]{1,0:T(8,128)(2,1)S(1)} %fusion.30), channel_id=1, source_target_pairs={{0,4},{4,8},{8,12},{12,16},{16,20},{20,24},{24,28},{28,0},{1,5},{5... | collective-permute-start | bytes 147464 | tf_op jit(solution)/shard_map/ppermute | solution.py:9
  151.3 15.3 %collective-permute-start.36 = (bf16[2048,128]{0,1:T(8,128)(2,1)S(1)}, bf16[2048,128]{0,1:T(8,128)(2,1)S(1)}, u32[]{:S(2)}, u32[]{:S(2)}) collective-permute-start(bf16[2048,128]{0,1:T(8,128)(2,1)S(1)} %fusion.13), channel_id=1, source_target_pairs={{0,1},{1,0},{2,3},{3,2},{4,5},{5,4},{6,7},{7,6},{8,9},{9,8},{10,11... | collective-permute-start | bytes 1572872 | tf_op jit(solution)/shard_map/ppermute | solution.py:14
  166.7 13.2 %collective-permute-start.37 = (bf16[2048,128]{0,1:T(8,128)(2,1)S(1)}, bf16[2048,128]{0,1:T(8,128)(2,1)S(1)}, u32[]{:S(2)}, u32[]{:S(2)}) collective-permute-start(bf16[2048,128]{0,1:T(8,128)(2,1)S(1)} %fusion.10), channel_id=1, source_target_pairs={{0,2},{1,3},{2,0},{3,1},{4,6},{5,7},{6,4},{7,5},{8,10},{9,11},{10,... | collective-permute-start | bytes 1572872 | tf_op jit(solution)/shard_map/ppermute | solution.py:14
  167.0 12.9 %collective-permute-start.39 = (f32[128]{0:T(128)S(1)}, f32[128]{0:T(128)S(1)}, u32[]{:S(2)}, u32[]{:S(2)}) collective-permute-start(f32[128]{0:T(128)S(1)} %add.376), channel_id=1, source_target_pairs={{0,2},{1,3},{2,0},{3,1},{4,6},{5,7},{6,4},{7,5},{8,10},{9,11},{10,... | collective-permute-start | bytes 1544 | tf_op jit(solution)/shard_map/ppermute | solution.py:14
  211.6 7.5 %collective-permute-start.55 = (bf16[2048,128]{0,1:T(8,128)(2,1)S(1)}, bf16[2048,128]{0,1:T(8,128)(2,1)S(1)}, u32[]{:S(2)}, u32[]{:S(2)}) collective-permute-start(bf16[2048,128]{0,1:T(8,128)(2,1)S(1)} %fusion.14), channel_id=1, source_target_pairs={{0,1},{1,0},{2,3},{3,2},{4,5},{5,4},{6,7},{7,6},{8,9},{9,8},{10,11... | collective-permute-start | bytes 1572872 | tf_op jit(solution)/shard_map/ppermute | solution.py:14
  219.1 13.2 %collective-permute-start.56 = (bf16[2048,128]{0,1:T(8,128)(2,1)S(1)}, bf16[2048,128]{0,1:T(8,128)(2,1)S(1)}, u32[]{:S(2)}, u32[]{:S(2)}) collective-permute-start(bf16[2048,128]{0,1:T(8,128)(2,1)S(1)} %fusion.9), channel_id=1, source_target_pairs={{0,2},{1,3},{2,0},{3,1},{4,6},{5,7},{6,4},{7,5},{8,10},{9,11},{10,... | collective-permute-start | bytes 1572872 | tf_op jit(solution)/shard_map/ppermute | solution.py:14
  219.4 12.9 %collective-permute-start.58 = (f32[128]{0:T(128)S(1)}, f32[128]{0:T(128)S(1)}, u32[]{:S(2)}, u32[]{:S(2)}) collective-permute-start(f32[128]{0:T(128)S(1)} %add.387), channel_id=1, source_target_pairs={{0,2},{1,3},{2,0},{3,1},{4,6},{5,7},{6,4},{7,5},{8,10},{9,11},{10,... | collective-permute-start | bytes 1544 | tf_op jit(solution)/shard_map/ppermute | solution.py:14
  233.3 16.1 %collective-permute-start.59 = (bf16[2048,128]{0,1:T(8,128)(2,1)}, bf16[2048,128]{0,1:T(8,128)(2,1)}, u32[]{:S(2)}, u32[]{:S(2)}) collective-permute-start(bf16[2048,128]{0,1:T(8,128)(2,1)} %divide_convert_fusion), channel_id=1, source_target_pairs={{0,1},{1,0},{2,3},{3,2},{4,5},{5,4},{6,7},{7,6},{8,9},{9,8},{10,11... | collective-permute-start | bytes 1572872 | tf_op jit(solution)/shard_map/ppermute | solution.py:14
  (60 other events, 433.7 us)

commit v2 on v0

v2 whole, which is shorter than its diff:
```python
import functools

import jax
import jax.numpy as jnp
from jax import lax
from jax.experimental import pallas as pl
from jax.experimental.pallas import tpu as pltpu
from jax.sharding import PartitionSpec as P

F32 = jnp.float32
BF16 = jnp.bfloat16


def swap(value, axis, bit):
    count = lax.axis_size(axis)
    return lax.ppermute(value, axis, [(i, i ^ bit) for i in range(count)])


def dot_nt(a, b):
    return lax.dot_general(a, b, (((1,), (1,)), ((), ())), preferred_element_type=F32)


def dot_tn(a, b):
    return lax.dot_general(a, b, (((0,), (0,)), ((), ())), preferred_element_type=F32)


def first_kernel(words, emb, norm, beta, right, weighted, proj):
    emit = jnp.exp(dot_nt(words[...], emb[...]) - norm[...])
    value = (emit * beta[...].astype(F32).T).astype(BF16)
    weighted[...] = value

    @pl.when(pl.program_id(0) == 0)
    def _():
        proj[...] = jnp.zeros_like(proj)

    proj[...] += jnp.dot(value, right[...], preferred_element_type=F32)


def first_weighted(words, emb, norm, beta, right, tile):
    states, width = emb.shape
    batch = words.shape[0]
    columns = right.shape[1]
    return pl.pallas_call(
        first_kernel,
        grid=(states // tile,),
        in_specs=[
            pl.BlockSpec((batch, width), lambda i: (0, 0)),
            pl.BlockSpec((tile, width), lambda i: (i, 0)),
            pl.BlockSpec((1, tile), lambda i: (0, i)),
            pl.BlockSpec((tile, batch), lambda i: (i, 0)),
            pl.BlockSpec((tile, columns), lambda i: (i, 0)),
        ],
        out_specs=[
            pl.BlockSpec((batch, tile), lambda i: (0, i)),
            pl.BlockSpec((batch, columns), lambda i: (0, 0)),
        ],
        out_shape=[
            jax.ShapeDtypeStruct((batch, states), BF16),
            jax.ShapeDtypeStruct((batch, columns), F32),
        ],
        cost_estimate=pl.CostEstimate(
            flops=2 * states * batch * (columns + width),
            bytes_accessed=2 * states * (columns + width + 2 * batch),
            transcendentals=states * batch,
        ),
        name="first_weighted",
    )(words, emb, norm, beta, right)


def prepare_kernel(left, words, emb, norm, flipped, sums, emit):
    block = left[...]
    flipped[...] = block.T
    emit[...] = jnp.exp(dot_nt(words[...], emb[...]) - norm[...])

    @pl.when(pl.program_id(0) == 0)
    def _():
        sums[...] = jnp.zeros_like(sums)

    sums[...] += jnp.broadcast_to(
        jnp.sum(block.astype(F32), axis=0, keepdims=True), sums.shape
    )


def prepare(left, words, emb, norm, tile):
    states, columns = left.shape
    rows, width = words.shape
    return pl.pallas_call(
        prepare_kernel,
        grid=(states // tile,),
        in_specs=[
            pl.BlockSpec((tile, columns), lambda i: (i, 0)),
            pl.BlockSpec((rows, width), lambda i: (0, 0)),
            pl.BlockSpec((tile, width), lambda i: (i, 0)),
            pl.BlockSpec((1, tile), lambda i: (0, i)),
        ],
        out_specs=[
            pl.BlockSpec((columns, tile), lambda i: (0, i)),
            pl.BlockSpec((16, columns), lambda i: (0, 0)),
            pl.BlockSpec((rows, tile), lambda i: (0, i)),
        ],
        out_shape=[
            jax.ShapeDtypeStruct((columns, states), BF16),
            jax.ShapeDtypeStruct((16, columns), F32),
            jax.ShapeDtypeStruct((rows, states), F32),
        ],
        cost_estimate=pl.CostEstimate(
            flops=2 * states * rows * width,
            bytes_accessed=states * (4 * columns + 4 * rows + 2 * width),
            transcendentals=states * rows,
        ),
        name="prepare",
    )(left, words, emb, norm)


def grads_kernel(scale, marg, proj, fwd, *refs):
    weighted, (grad_left, grad_right) = refs[:-2], refs[-2:]
    grad_left[...] = (
        jnp.dot(marg[...], proj[...], preferred_element_type=F32) * scale
    ).astype(BF16)
    rows = jnp.concatenate([ref[...] for ref in weighted], axis=0)
    grad_right[...] = (dot_tn(rows, fwd[...]) * scale).astype(BF16)


def gradients(marg, proj, fwd, weighted, tile):
    states, rows = marg.shape
    columns = proj.shape[1]
    return pl.pallas_call(
        functools.partial(grads_kernel, 1.0 / rows),
        grid=(states // tile,),
        in_specs=[
            pl.BlockSpec((tile, rows), lambda i: (i, 0)),
            pl.BlockSpec((rows, columns), lambda i: (0, 0)),
            pl.BlockSpec((rows, columns), lambda i: (0, 0)),
        ]
        + [pl.BlockSpec((w.shape[0], tile), lambda i: (0, i)) for w in weighted],
        out_specs=[pl.BlockSpec((tile, columns), lambda i: (i, 0))] * 2,
        out_shape=[jax.ShapeDtypeStruct((states, columns), BF16)] * 2,
        cost_estimate=pl.CostEstimate(
            flops=4 * states * rows * columns,
            bytes_accessed=4 * states * (rows + columns),
            transcendentals=0,
        ),
        name="gradients",
    )(marg, proj, fwd, *weighted)


def flip_kernel(first, second, out):
    out[...] = jnp.concatenate([first[...], second[...]], axis=0).astype(F32).T.astype(BF16)


def flip(first, second, tile):
    half, states = first.shape
    return pl.pallas_call(
        flip_kernel,
        grid=(states // tile,),
        in_specs=[pl.BlockSpec((half, tile), lambda i: (0, i))] * 2,
        out_specs=pl.BlockSpec((tile, 2 * half), lambda i: (i, 0)),
        out_shape=jax.ShapeDtypeStruct((states, 2 * half), BF16),
        name="flip",
    )(first, second)


def sum_over_state(keep, sent, extra=None):
    half = keep.shape[0]
    total = keep + swap(sent.astype(BF16), "state", 1).astype(F32)
    if extra is not None:
        total = jnp.concatenate([total, extra], axis=0)
    bit = 2
    while bit < lax.axis_size("state"):
        total = total + swap(total.astype(BF16), "state", bit).astype(F32)
        bit *= 2
    mine = total[:half].astype(BF16)
    if extra is None:
        return mine, swap(mine, "state", 1), None
    extra = total[half:]
    got = swap(jnp.concatenate([mine, extra.astype(BF16)], axis=0), "state", 1)
    return mine, got[:half], extra + got[half:].astype(F32)


def on_device(
    token_ids, word_emb, state_emb, log_norm, beta_last, forward_marg, trans_left, trans_right
):
    steps, batch = token_ids.shape
    half = batch // 2
    states = state_emb.shape[0]
    states_all = lax.axis_size("state") * states
    tile = 512
    low = lax.axis_index("rank") % 2
    side = lax.axis_index("state") % 2
    same = low == side

    words = word_emb.at[token_ids.reshape(-1)].get(mode="promise_in_bounds")
    norm = log_norm.reshape(1, states)
    last = (steps - 1) * batch
    weighted, proj_part = first_weighted(
        words[last:], state_emb, norm, beta_last, trans_right, tile
    )
    flipped, column_sums, emit_all = prepare(trans_left, words[:last], state_emb, norm, tile)

    def take_half(value, which):
        return lax.dynamic_slice_in_dim(value, which * half, half, 0)

    keep, sent = take_half(proj_part, side), take_half(proj_part, 1 - side)
    pieces = {steps - 1: [weighted[:half], weighted[half:]]}
    order = {steps - 1: [0, 1]}
    proj_rows = {}
    fwd = None
    beta = None
    for step in reversed(range(steps)):
        if step == steps - 1:
            mine, got, sums = sum_over_state(keep, sent, column_sums)
            column_sums = sums[:1]
        else:
            mine, got, _ = sum_over_state(keep, sent)
        proj_own = jnp.where(same, mine, got)
        proj_mate = jnp.where(same, got, mine)
        proj_rows[step] = [
            jnp.where(side == 0, mine, got),
            jnp.where(side == 0, got, mine),
        ]
        mass = jnp.sum(proj_own.astype(F32) * column_sums, axis=1)
        mass_mate = jnp.sum(proj_mate.astype(F32) * column_sums, axis=1)
        mass = mass + swap(mass_mate, "rank", 1)
        bit = 2
        while bit < lax.axis_size("rank"):
            mass = mass + swap(mass, "rank", bit)
            bit *= 2
        raw_mate = jnp.dot(proj_mate, flipped, preferred_element_type=F32).astype(BF16)
        raw_got = swap(raw_mate, "rank", 1)
        raw_own = jnp.dot(proj_own, flipped, preferred_element_type=F32)
        raw = raw_own + raw_got.astype(F32)
        bit = 2
        while bit < lax.axis_size("rank"):
            raw, mass = lax.optimization_barrier((raw, mass))
            raw = lax.reduce_precision(raw, 8, 7)
            raw = raw + swap(raw.astype(BF16), "rank", bit).astype(F32)
            bit *= 2
        scaled = raw * (states_all / mass)[:, None]
        if fwd is None:
            fwd_part = dot_tn(forward_marg, trans_left)
            rows = fwd_part.shape[0] // 2
            fwd_mine, fwd_got, _ = sum_over_state(
                lax.dynamic_slice_in_dim(fwd_part, side * rows, rows, 0) / states_all,
                lax.dynamic_slice_in_dim(fwd_part, (1 - side) * rows, rows, 0) / states_all,
            )
            fwd = jnp.concatenate(
                [
                    jnp.where(side == 0, fwd_mine, fwd_got),
                    jnp.where(side == 0, fwd_got, fwd_mine),
                ],
                axis=0,
            )
        if step == 0:
            beta_own = scaled.astype(BF16)
            beta_mate = swap(beta_own, "rank", 1)
            first = jnp.where(low == 0, beta_own, beta_mate)
            second = jnp.where(low == 0, beta_mate, beta_own)
            beta = flip(first, second, tile)
            break
        emit = lax.dynamic_slice_in_dim(
            emit_all, (step - 1) * batch + low * half, half, 0
        )
        own = (emit * scaled).astype(BF16)
        mate = swap(own, "rank", 1)
        part_own = jnp.dot(own, trans_right, preferred_element_type=F32)
        part_mate = jnp.dot(mate, trans_right, preferred_element_type=F32)
        keep = jnp.where(same, part_own, part_mate)
        sent = jnp.where(same, part_mate, part_own)
        pieces[step - 1] = [own, mate]
        order[step - 1] = [low, 1 - low]

    proj_all = jnp.concatenate([p for step in range(steps) for p in proj_rows[step]], axis=0)
    weighted_list, fwd_list = [], []
    for step in range(steps):
        for piece, place in zip(pieces[step], order[step]):
            weighted_list.append(piece)
            fwd_list.append(
                lax.dynamic_slice_in_dim(fwd, step * batch + place * half, half, 0)
            )
    grad_left, grad_right = gradients(
        forward_marg, proj_all, jnp.concatenate(fwd_list, axis=0), weighted_list, tile
    )
    return (beta, grad_left, grad_right)


def solution(mesh):
    placed = (
        P(),
        P(),
        P("state", None),
        P("state"),
        P("state", None),
        P("state", None),
        P("state", "rank"),
        P("state", "rank"),
    )
    return jax.shard_map(
        on_device,
        mesh=mesh,
        in_specs=placed,
        out_specs=(P("state", None), P("state", "rank"), P("state", "rank")),
        check_vma=False,
    )
```

time: 363 us -> 190 us (0.52)
  blocking collectives: 237 us -> 0 us
  starting transfers between devices: 0.16 us -> 47.3 us
  Pallas kernels: 0 us -> 32 us
  matrix products: 44.3 us -> 17.7 us
  waiting for transfers between devices: 37 us -> 60.6 us
  other arithmetic: 6.5 us -> 20.7 us
  local copies, waits for them, and re-layouts: 22 us -> 8.46 us
  between operations: 13.9 us -> 1.21 us
    psum x6 -> x0, blocking collectives: 237 us -> none  [the longest x3 135 us: on_device(): lax.psum(jnp.dot(projb.astype(jnp.float32), local_columns), ('state', 'ra...]
    ppermute x0 -> x31, waiting for transfers between devices: none -> 60.6 us  [swap(): return lax.ppermute(value, axis, [(i, i ^ bit) for i in range(count)])]
    ppermute x0 -> x31, starting transfers between devices: none -> 47.3 us  [swap(): return lax.ppermute(value, axis, [(i, i ^ bit) for i in range(count)])]
    psum x4 -> x0, waiting for transfers between devices: 36.9 us -> none  [the longest x3 36.9 us: on_device(): raw = lax.psum(raw_part, 'rank')]
    pallas_call x0 -> x4, Pallas kernels: none -> 32 us  [the longest x1 9.83 us: gradients(): pl.pallas_call(functools.partial(grads_kernel, 1.0 / rows), grid=(states...]
    dot_general x15 -> x11, matrix products: 44.3 us -> 17.7 us  [the longest x3 6.99 us: on_device(): jnp.dot(proj_mate, flipped, preferred_element_type=F32).astype(BF16)]
    convert_element_type x1 -> x18, other arithmetic: 2.8 us -> 13.5 us  [the longest x8 5.03 us: sum_over_state(): total = total + swap(total.astype(BF16), 'state', bit).astype(F32)]
    unnamed x17 -> x46, local copies, waits for them, and re-layouts: 13.9 us -> 3.7 us
  transfers between devices with their start and end apart: 4 -> 31, of which waited for: 3 -> 21; matrix products, arithmetic and copies ran while one was open for 11% -> 13% of each run, Pallas kernels for 0% -> 10%
where the time goes in v2:
time: 190 us; the launch traced here: 188 us
  waiting for transfers between devices  60.6 us (32%)
  starting transfers between devices  47.3 us (25%)
  Pallas kernels  32 us (17%)
  other arithmetic  20.7 us (11%)
  matrix products  17.7 us (9%)
  local copies, waits for them, and re-layouts  8.46 us (4%)
    ppermute x31, waiting for transfers between devices, swap(): return lax.ppermute(value, axis, [(i, i ^ bit) for i in range(count)])  60.6 us
    ppermute x31, starting transfers between devices, swap(): return lax.ppermute(value, axis, [(i, i ^ bit) for i in range(count)])  47.3 us
    pallas_call x1, Pallas kernels, gradients(): pl.pallas_call(functools.partial(grads_kernel, 1.0 / rows), grid=(states...  9.83 us
    pallas_call x1, Pallas kernels, prepare(): pl.pallas_call(prepare_kernel, grid=(states // tile,), in_specs=[pl.Block...  8.86 us
    pallas_call x1, Pallas kernels, first_weighted(): pl.pallas_call(first_kernel, grid=(states // tile,), in_specs=[pl.BlockSp...  7.97 us
    dot_general x3, matrix products, on_device(): jnp.dot(proj_mate, flipped, preferred_element_type=F32).astype(BF16)  6.99 us
    pallas_call x1, Pallas kernels, flip(): pl.pallas_call(flip_kernel, grid=(states // tile,), in_specs=[pl.BlockSpe...  5.39 us
    convert_element_type x8, other arithmetic, sum_over_state(): total = total + swap(total.astype(BF16), 'state', bit).astype(F32)  5.03 us
  transfers between devices with their start and end apart: 31, of which 21 were waited for; matrix products, arithmetic and copies ran while one was open for 13% of the time, Pallas kernels for 10%

profile of v2, /device:TPU:1, one launch (start us, length us, event | category | flops | bytes accessed | tf_op | source)
XLA Modules:
  0.0 188.1 jit_solution(6080498255132373039)
XLA Ops:
  4.4 8.0 %first_weighted.1 = (bf16[128,4096]{1,0:T(8,128)(2,1)}, f32[128,512]{1,0:T(8,128)}) custom-call(bf16[128,128]{1,0:T(8,128)(2,1)} %slice.41.words, bf16[4096,128]{1,0:T(8,128)(2,1)} %emb.3, f32[1,4096]{1,0:T(1,128)} %bitcast.23, bf16[4096,128]{1,0:T(8,128)(2,1)} %beta.1, bf16[4096,512]{1,0:T(8,128)(2,1)} %right.1), custom_call_target="tpu_custom_call" | custom-call | flops 671088640 | bytes 7340032 | tf_op jit(solution)/shard_map/first_weighted/pallas_call | solution.py:43
  16.1 8.9 %prepare.1 = (bf16[512,4096]{1,0:T(8,128)(2,1)}, f32[16,512]{1,0:T(8,128)}, f32[256,4096]{1,0:T(8,128)}) custom-call(bf16[4096,512]{1,0:T(8,128)(2,1)} %left.1, bf16[256,128]{1,0:T(8,128)(2,1)} %slice.40.words, bf16[4096,128]{1,0:T(8,128)(2,1)} %emb.3, f32[1,4096]{1,0:T(1,128)} %bitcast.24), custom_call_target="tpu_custom_call" | custom-call | flops 268435456 | bytes 13631488 | tf_op jit(solution)/shard_map/prepare/pallas_call | solution.py:87
  30.0 2.4 %collective-permute-start.2 = (bf16[80,512]{1,0:T(8,128)(2,1)S(1)}, bf16[80,512]{1,0:T(8,128)(2,1)S(1)}, u32[]{:S(2)}, u32[]{:S(2)}) collective-permute-start(bf16[80,512]{1,0:T(8,128)(2,1)S(1)} %fusion.4), channel_id=1, source_target_pairs={{0,16},{4,20},{8,24},{12,28},{16,0},{20,4},{24,8},{28,12},{1,17},{... | collective-permute-start | bytes 245768 | tf_op jit(solution)/shard_map/ppermute | solution.py:16
  35.3 3.1 %collective-permute-done.3 = bf16[80,512]{1,0:T(8,128)(2,1)S(1)} collective-permute-done((bf16[80,512]{1,0:T(8,128)(2,1)S(1)}, bf16[80,512]{1,0:T(8,128)(2,1)S(1)}, u32[]{:S(2)}, u32[]{:S(2)}) %collective-permute-start.3) | collective-permute-done | bytes 81952 | tf_op jit(solution)/shard_map/ppermute | solution.py:16
  38.4 3.1 %convolution_convert_fusion.2 = bf16[64,4096]{1,0:T(8,128)(2,1)S(1)} fusion(bf16[512,4096]{1,0:T(8,128)(2,1)} %get-tuple-element.19, pred[]{:T(512)S(6)} %eq.10, bf16[80,512]{1,0:T(8,128)(2,1)S(1)} %collective-permute-done.3, f32[80,512]{1,0:T(8,128)S(1)} %convert_add_fusion.2), kind=kOutput, calls=%fused_computation.6 | convolution fusion | flops 268730368 | bytes 4849665 | tf_op jit(solution)/shard_map/dot_general | solution.py:228
  41.5 4.5 %collective-permute-start.4 = (bf16[64,4096]{1,0:T(8,128)(2,1)S(1)}, bf16[64,4096]{1,0:T(8,128)(2,1)S(1)}, u32[]{:S(2)}, u32[]{:S(2)}) collective-permute-start(bf16[64,4096]{1,0:T(8,128)(2,1)S(1)} %convolution_convert_fusion.2), channel_id=1, source_target_pairs={{0,1},{1,0},{2,3},{3,2},{4,5},{5,4},{6,7},{7,6},{8,9},{9,8},{10,11... | collective-permute-start | bytes 1572872 | tf_op jit(solution)/shard_map/ppermute | solution.py:16
  53.2 10.8 %collective-permute-done.7 = bf16[64,4096]{1,0:T(8,128)(2,1)} collective-permute-done((bf16[64,4096]{1,0:T(8,128)(2,1)S(1)}, bf16[64,4096]{1,0:T(8,128)(2,1)}, u32[]{:S(2)}, u32[]{:S(2)}) %collective-permute-start.7) | collective-permute-done | bytes 524320 | tf_op jit(solution)/shard_map/ppermute | solution.py:16
  65.8 2.5 %collective-permute-start.8 = (bf16[64,4096]{1,0:T(8,128)(2,1)S(1)}, bf16[64,4096]{1,0:T(8,128)(2,1)S(1)}, u32[]{:S(2)}, u32[]{:S(2)}) collective-permute-start(bf16[64,4096]{1,0:T(8,128)(2,1)S(1)} %multiply_convert_fusion.2.refs_2_), channel_id=1, source_target_pairs={{0,1},{1,0},{2,3},{3,2},{4,5},{5,4},{6,7},{7,6},{8,9},{9,8},{10,11... | collective-permute-start | bytes 1572872 | tf_op jit(solution)/shard_map/ppermute | solution.py:16
  68.4 3.0 %fusion.20 = f32[64,512]{1,0:T(8,128)S(1)} fusion(bf16[64,4096]{1,0:T(8,128)(2,1)S(1)} %multiply_convert_fusion.2.refs_2_, bf16[4096,512]{1,0:T(8,128)(2,1)} %right.1), kind=kOutput, calls=%fused_computation.91 | convolution fusion | flops 268435456 | bytes 4849664 | tf_op jit(solution)/shard_map/dot_general | solution.py:265
  72.4 3.1 %collective-permute-done.9 = bf16[64,512]{1,0:T(8,128)(2,1)S(1)} collective-permute-done((bf16[64,512]{1,0:T(8,128)(2,1)S(1)}, bf16[64,512]{1,0:T(8,128)(2,1)S(1)}, u32[]{:S(2)}, u32[]{:S(2)}) %collective-permute-start.9) | collective-permute-done | bytes 65568 | tf_op jit(solution)/shard_map/ppermute | solution.py:16
  79.3 3.0 %collective-permute-start.11 = (bf16[64,512]{1,0:T(8,128)(2,1)}, bf16[64,512]{1,0:T(8,128)(2,1)}, u32[]{:S(2)}, u32[]{:S(2)}) collective-permute-start(bf16[64,512]{1,0:T(8,128)(2,1)} %fusion.2), channel_id=1, source_target_pairs={{0,16},{4,20},{8,24},{12,28},{16,0},{20,4},{24,8},{28,12},{1,17},{... | collective-permute-start | bytes 196616 | tf_op jit(solution)/shard_map/ppermute | solution.py:16
  89.3 3.1 %convolution_convert_fusion.1 = bf16[64,4096]{1,0:T(8,128)(2,1)S(1)} fusion(bf16[512,4096]{1,0:T(8,128)(2,1)} %get-tuple-element.19, bf16[64,512]{1,0:T(8,128)(2,1)} %collective-permute-done.12, bf16[64,512]{1,0:T(8,128)(2,1)} %add_convert_fusion.2, pred[]{:T(512)S(6)} %eq.10), kind=kOutput, calls=%fused_computation.5 | convolution fusion | flops 268730368 | bytes 4849665 | tf_op jit(solution)/shard_map/dot_general | solution.py:228
  92.4 4.4 %collective-permute-start.13 = (bf16[64,4096]{1,0:T(8,128)(2,1)S(1)}, bf16[64,4096]{1,0:T(8,128)(2,1)S(1)}, u32[]{:S(2)}, u32[]{:S(2)}) collective-permute-start(bf16[64,4096]{1,0:T(8,128)(2,1)S(1)} %convolution_convert_fusion.1), channel_id=1, source_target_pairs={{0,1},{1,0},{2,3},{3,2},{4,5},{5,4},{6,7},{7,6},{8,9},{9,8},{10,11... | collective-permute-start | bytes 1572872 | tf_op jit(solution)/shard_map/ppermute | solution.py:16
  106.5 2.8 %collective-permute-start.29 = (bf16[192,512]{1,0:T(8,128)(2,1)}, bf16[192,512]{1,0:T(8,128)(2,1)}, u32[]{:S(2)}, u32[]{:S(2)}) collective-permute-start(bf16[192,512]{1,0:T(8,128)(2,1)} %fusion), channel_id=1, source_target_pairs={{0,16},{4,20},{8,24},{12,28},{16,0},{20,4},{24,8},{28,12},{1,17},{... | collective-permute-start | bytes 589832 | tf_op jit(solution)/shard_map/ppermute | solution.py:16
  115.2 3.3 %collective-permute-done.29 = bf16[192,512]{1,0:T(8,128)(2,1)} collective-permute-done((bf16[192,512]{1,0:T(8,128)(2,1)}, bf16[192,512]{1,0:T(8,128)(2,1)}, u32[]{:S(2)}, u32[]{:S(2)}) %collective-permute-start.29) | collective-permute-done | bytes 196640 | tf_op jit(solution)/shard_map/ppermute | solution.py:16
  119.9 5.9 %collective-permute-done.16 = bf16[64,4096]{1,0:T(8,128)(2,1)} collective-permute-done((bf16[64,4096]{1,0:T(8,128)(2,1)}, bf16[64,4096]{1,0:T(8,128)(2,1)}, u32[]{:S(2)}, u32[]{:S(2)}) %collective-permute-start.16) | collective-permute-done | bytes 524320 | tf_op jit(solution)/shard_map/ppermute | solution.py:16
  132.3 2.9 %collective-permute-done.18 = bf16[64,512]{1,0:T(8,128)(2,1)S(1)} collective-permute-done((bf16[64,512]{1,0:T(8,128)(2,1)S(1)}, bf16[64,512]{1,0:T(8,128)(2,1)S(1)}, u32[]{:S(2)}, u32[]{:S(2)}) %collective-permute-start.18) | collective-permute-done | bytes 65568 | tf_op jit(solution)/shard_map/ppermute | solution.py:16
  138.5 3.9 %collective-permute-done.20 = bf16[64,512]{1,0:T(8,128)(2,1)S(1)} collective-permute-done((bf16[64,512]{1,0:T(8,128)(2,1)S(1)}, bf16[64,512]{1,0:T(8,128)(2,1)S(1)}, u32[]{:S(2)}, u32[]{:S(2)}) %collective-permute-start.20) | collective-permute-done | bytes 65568 | tf_op jit(solution)/shard_map/ppermute | solution.py:16
  142.8 3.1 %collective-permute-done.21 = bf16[64,512]{1,0:T(8,128)(2,1)S(1)} collective-permute-done((bf16[64,512]{1,0:T(8,128)(2,1)S(1)}, bf16[64,512]{1,0:T(8,128)(2,1)S(1)}, u32[]{:S(2)}, u32[]{:S(2)}) %collective-permute-start.21) | collective-permute-done | bytes 65568 | tf_op jit(solution)/shard_map/ppermute | solution.py:16
  146.0 4.8 %collective-permute-start.23 = (f32[64]{0:T(128)S(1)}, f32[64]{0:T(128)S(1)}, u32[]{:S(2)}, u32[]{:S(2)}) collective-permute-start(f32[64]{0:T(128)S(1)} %get-tuple-element.31), channel_id=1, source_target_pairs={{0,1},{1,0},{2,3},{3,2},{4,5},{5,4},{6,7},{7,6},{8,9},{9,8},{10,11... | collective-permute-start | bytes 776 | tf_op jit(solution)/shard_map/ppermute | solution.py:16
  157.5 9.6 %collective-permute-done.25 = bf16[64,4096]{1,0:T(8,128)(2,1)S(1)} collective-permute-done((bf16[64,4096]{1,0:T(8,128)(2,1)S(1)}, bf16[64,4096]{1,0:T(8,128)(2,1)S(1)}, u32[]{:S(2)}, u32[]{:S(2)}) %collective-permute-start.25) | collective-permute-done | bytes 524320 | tf_op jit(solution)/shard_map/ppermute | solution.py:16
  167.3 2.6 %collective-permute-start.26 = (bf16[64,4096]{1,0:T(8,128)(2,1)S(1)}, bf16[64,4096]{1,0:T(8,128)(2,1)}, u32[]{:S(2)}, u32[]{:S(2)}) collective-permute-start(bf16[64,4096]{1,0:T(8,128)(2,1)S(1)} %multiply_convert_fusion), channel_id=1, source_target_pairs={{0,1},{1,0},{2,3},{3,2},{4,5},{5,4},{6,7},{7,6},{8,9},{9,8},{10,11... | collective-permute-start | bytes 1572872 | tf_op jit(solution)/shard_map/ppermute | solution.py:16
  170.7 9.8 %gradients.1 = (bf16[4096,512]{1,0:T(8,128)(2,1)}, bf16[4096,512]{1,0:T(8,128)(2,1)}) custom-call(bf16[4096,384]{1,0:T(8,128)(2,1)} %marg.1, bf16[384,512]{1,0:T(8,128)(2,1)} %copy-done.20, bf16[384,512]{1,0:T(8,128)(2,1)} %copy-done.21, bf16[64,4096]{1,0:T(8,128)(2,1)} %copy-done.10, bf16[64,4096]{1,0:T(8,128)(2,1)} %copy-done.17, ...), custom_call_target="tpu_custom_call" | custom-call | flops 3221225472 | bytes 14680064 | tf_op jit(solution)/shard_map/gradients/pallas_call | solution.py:127
  182.7 5.4 %flip.1 = bf16[4096,128]{1,0:T(8,128)(2,1)} custom-call(bf16[64,4096]{1,0:T(8,128)(2,1)} %get-tuple-element.42.first, bf16[64,4096]{1,0:T(8,128)(2,1)} %get-tuple-element.41.second), custom_call_target="tpu_custom_call" | custom-call | tf_op jit(solution)/shard_map/flip/pallas_call | solution.py:153
  (157 shorter events, 73.0 us)
Async XLA Ops:
  13.4 11.6 %collective-permute-start = (bf16[64,512]{1,0:T(8,128)(2,1)S(1)}, bf16[64,512]{1,0:T(8,128)(2,1)S(1)}, u32[]{:S(2)}, u32[]{:S(2)}) collective-permute-start(bf16[64,512]{1,0:T(8,128)(2,1)S(1)} %dynamic-slice_convert_fusion), channel_id=1, source_target_pairs={{0,4},{4,0},{8,12},{12,8},{16,20},{20,16},{24,28},{28,24},{1,5},{5... | collective-permute-start | bytes 196616 | tf_op jit(solution)/shard_map/ppermute | solution.py:16
  25.8 3.4 %collective-permute-start.1 = (bf16[80,512]{1,0:T(8,128)(2,1)S(1)}, bf16[80,512]{1,0:T(8,128)(2,1)S(1)}, u32[]{:S(2)}, u32[]{:S(2)}) collective-permute-start(bf16[80,512]{1,0:T(8,128)(2,1)S(1)} %fusion.1), channel_id=1, source_target_pairs={{0,8},{4,12},{8,0},{12,4},{16,24},{20,28},{24,16},{28,20},{1,9},{5... | collective-permute-start | bytes 245768 | tf_op jit(solution)/shard_map/ppermute | solution.py:16
  30.0 4.3 %collective-permute-start.2 = (bf16[80,512]{1,0:T(8,128)(2,1)S(1)}, bf16[80,512]{1,0:T(8,128)(2,1)S(1)}, u32[]{:S(2)}, u32[]{:S(2)}) collective-permute-start(bf16[80,512]{1,0:T(8,128)(2,1)S(1)} %fusion.4), channel_id=1, source_target_pairs={{0,16},{4,20},{8,24},{12,28},{16,0},{20,4},{24,8},{28,12},{1,17},{... | collective-permute-start | bytes 245768 | tf_op jit(solution)/shard_map/ppermute | solution.py:16
  35.0 3.4 %collective-permute-start.3 = (bf16[80,512]{1,0:T(8,128)(2,1)S(1)}, bf16[80,512]{1,0:T(8,128)(2,1)S(1)}, u32[]{:S(2)}, u32[]{:S(2)}) collective-permute-start(bf16[80,512]{1,0:T(8,128)(2,1)S(1)} %pad_maximum_fusion.1), channel_id=1, source_target_pairs={{0,4},{4,0},{8,12},{12,8},{16,20},{20,16},{24,28},{28,24},{1,5},{5... | collective-permute-start | bytes 245768 | tf_op jit(solution)/shard_map/ppermute | solution.py:16
  41.5 8.4 %collective-permute-start.4 = (bf16[64,4096]{1,0:T(8,128)(2,1)S(1)}, bf16[64,4096]{1,0:T(8,128)(2,1)S(1)}, u32[]{:S(2)}, u32[]{:S(2)}) collective-permute-start(bf16[64,4096]{1,0:T(8,128)(2,1)S(1)} %convolution_convert_fusion.2), channel_id=1, source_target_pairs={{0,1},{1,0},{2,3},{3,2},{4,5},{5,4},{6,7},{7,6},{8,9},{9,8},{10,11... | collective-permute-start | bytes 1572872 | tf_op jit(solution)/shard_map/ppermute | solution.py:16
  51.8 12.1 %collective-permute-start.7 = (bf16[64,4096]{1,0:T(8,128)(2,1)S(1)}, bf16[64,4096]{1,0:T(8,128)(2,1)}, u32[]{:S(2)}, u32[]{:S(2)}) collective-permute-start(bf16[64,4096]{1,0:T(8,128)(2,1)S(1)} %reduce-precision_convert_fusion.2), channel_id=1, source_target_pairs={{0,2},{1,3},{2,0},{3,1},{4,6},{5,7},{6,4},{7,5},{8,10},{9,11},{10,... | collective-permute-start | bytes 1572872 | tf_op jit(solution)/shard_map/ppermute | solution.py:16
  65.8 5.5 %collective-permute-start.8 = (bf16[64,4096]{1,0:T(8,128)(2,1)S(1)}, bf16[64,4096]{1,0:T(8,128)(2,1)S(1)}, u32[]{:S(2)}, u32[]{:S(2)}) collective-permute-start(bf16[64,4096]{1,0:T(8,128)(2,1)S(1)} %multiply_convert_fusion.2.refs_2_), channel_id=1, source_target_pairs={{0,1},{1,0},{2,3},{3,2},{4,5},{5,4},{6,7},{7,6},{8,9},{9,8},{10,11... | collective-permute-start | bytes 1572872 | tf_op jit(solution)/shard_map/ppermute | solution.py:16
  72.3 3.2 %collective-permute-start.9 = (bf16[64,512]{1,0:T(8,128)(2,1)S(1)}, bf16[64,512]{1,0:T(8,128)(2,1)S(1)}, u32[]{:S(2)}, u32[]{:S(2)}) collective-permute-start(bf16[64,512]{1,0:T(8,128)(2,1)S(1)} %get-tuple-element.45), channel_id=1, source_target_pairs={{0,4},{4,0},{8,12},{12,8},{16,20},{20,16},{24,28},{28,24},{1,5},{5... | collective-permute-start | bytes 196616 | tf_op jit(solution)/shard_map/ppermute | solution.py:16
  75.5 3.2 %collective-permute-start.10 = (bf16[64,512]{1,0:T(8,128)(2,1)S(1)}, bf16[64,512]{1,0:T(8,128)(2,1)S(1)}, u32[]{:S(2)}, u32[]{:S(2)}) collective-permute-start(bf16[64,512]{1,0:T(8,128)(2,1)S(1)} %get-tuple-element.37), channel_id=1, source_target_pairs={{0,8},{4,12},{8,0},{12,4},{16,24},{20,28},{24,16},{28,20},{1,9},{5... | collective-permute-start | bytes 196616 | tf_op jit(solution)/shard_map/ppermute | solution.py:16
  79.3 4.9 %collective-permute-start.11 = (bf16[64,512]{1,0:T(8,128)(2,1)}, bf16[64,512]{1,0:T(8,128)(2,1)}, u32[]{:S(2)}, u32[]{:S(2)}) collective-permute-start(bf16[64,512]{1,0:T(8,128)(2,1)} %fusion.2), channel_id=1, source_target_pairs={{0,16},{4,20},{8,24},{12,28},{16,0},{20,4},{24,8},{28,12},{1,17},{... | collective-permute-start | bytes 196616 | tf_op jit(solution)/shard_map/ppermute | solution.py:16
  85.8 3.4 %collective-permute-start.12 = (bf16[64,512]{1,0:T(8,128)(2,1)}, bf16[64,512]{1,0:T(8,128)(2,1)}, u32[]{:S(2)}, u32[]{:S(2)}) collective-permute-start(bf16[64,512]{1,0:T(8,128)(2,1)} %add_convert_fusion.2), channel_id=1, source_target_pairs={{0,4},{4,0},{8,12},{12,8},{16,20},{20,16},{24,28},{28,24},{1,5},{5... | collective-permute-start | bytes 196616 | tf_op jit(solution)/shard_map/ppermute | solution.py:16
  86.8 9.9 %collective-permute-start.27 = (bf16[192,512]{1,0:T(8,128)(2,1)}, bf16[192,512]{1,0:T(8,128)(2,1)}, u32[]{:S(2)}, u32[]{:S(2)}) collective-permute-start(bf16[192,512]{1,0:T(8,128)(2,1)} %multiply_convert_fusion.3), channel_id=1, source_target_pairs={{0,4},{4,0},{8,12},{12,8},{16,20},{20,16},{24,28},{28,24},{1,5},{5... | collective-permute-start | bytes 589832 | tf_op jit(solution)/shard_map/ppermute | solution.py:16
  92.4 17.0 %collective-permute-start.13 = (bf16[64,4096]{1,0:T(8,128)(2,1)S(1)}, bf16[64,4096]{1,0:T(8,128)(2,1)S(1)}, u32[]{:S(2)}, u32[]{:S(2)}) collective-permute-start(bf16[64,4096]{1,0:T(8,128)(2,1)S(1)} %convolution_convert_fusion.1), channel_id=1, source_target_pairs={{0,1},{1,0},{2,3},{3,2},{4,5},{5,4},{6,7},{7,6},{8,9},{9,8},{10,11... | collective-permute-start | bytes 1572872 | tf_op jit(solution)/shard_map/ppermute | solution.py:16
  97.7 7.0 %collective-permute-start.28 = (bf16[192,512]{1,0:T(8,128)(2,1)S(1)}, bf16[192,512]{1,0:T(8,128)(2,1)S(1)}, u32[]{:S(2)}, u32[]{:S(2)}) collective-permute-start(bf16[192,512]{1,0:T(8,128)(2,1)S(1)} %fusion.13), channel_id=1, source_target_pairs={{0,8},{4,12},{8,0},{12,4},{16,24},{20,28},{24,16},{28,20},{1,9},{5... | collective-permute-start | bytes 589832 | tf_op jit(solution)/shard_map/ppermute | solution.py:16
  101.7 7.6 %collective-permute-start.15 = (f32[64]{0:T(128)S(1)}, f32[64]{0:T(128)S(1)}, u32[]{:S(2)}, u32[]{:S(2)}) collective-permute-start(f32[64]{0:T(128)S(1)} %add.157), channel_id=1, source_target_pairs={{0,2},{1,3},{2,0},{3,1},{4,6},{5,7},{6,4},{7,5},{8,10},{9,11},{10,... | collective-permute-start | bytes 776 | tf_op jit(solution)/shard_map/ppermute | solution.py:16
  106.5 12.0 %collective-permute-start.29 = (bf16[192,512]{1,0:T(8,128)(2,1)}, bf16[192,512]{1,0:T(8,128)(2,1)}, u32[]{:S(2)}, u32[]{:S(2)}) collective-permute-start(bf16[192,512]{1,0:T(8,128)(2,1)} %fusion), channel_id=1, source_target_pairs={{0,16},{4,20},{8,24},{12,28},{16,0},{20,4},{24,8},{28,12},{1,17},{... | collective-permute-start | bytes 589832 | tf_op jit(solution)/shard_map/ppermute | solution.py:16
  112.9 12.9 %collective-permute-start.16 = (bf16[64,4096]{1,0:T(8,128)(2,1)}, bf16[64,4096]{1,0:T(8,128)(2,1)}, u32[]{:S(2)}, u32[]{:S(2)}) collective-permute-start(bf16[64,4096]{1,0:T(8,128)(2,1)} %reduce-precision_convert_fusion.1), channel_id=1, source_target_pairs={{0,2},{1,3},{2,0},{3,1},{4,6},{5,7},{6,4},{7,5},{8,10},{9,11},{10,... | collective-permute-start | bytes 1572872 | tf_op jit(solution)/shard_map/ppermute | solution.py:16
  119.8 9.8 %collective-permute-start.30 = (bf16[192,512]{1,0:T(8,128)(2,1)S(1)}, bf16[192,512]{1,0:T(8,128)(2,1)S(1)}, u32[]{:S(2)}, u32[]{:S(2)}) collective-permute-start(bf16[192,512]{1,0:T(8,128)(2,1)S(1)} %add_convert_fusion), channel_id=1, source_target_pairs={{0,4},{4,0},{8,12},{12,8},{16,20},{20,16},{24,28},{28,24},{1,5},{5... | collective-permute-start | bytes 589832 | tf_op jit(solution)/shard_map/ppermute | solution.py:16
  127.7 3.4 %collective-permute-start.17 = (bf16[64,4096]{1,0:T(8,128)(2,1)S(1)}, bf16[64,4096]{1,0:T(8,128)(2,1)S(1)}, u32[]{:S(2)}, u32[]{:S(2)}) collective-permute-start(bf16[64,4096]{1,0:T(8,128)(2,1)S(1)} %multiply_convert_fusion.1.refs_0_), channel_id=1, source_target_pairs={{0,1},{1,0},{2,3},{3,2},{4,5},{5,4},{6,7},{7,6},{8,9},{9,8},{10,11... | collective-permute-start | bytes 1572872 | tf_op jit(solution)/shard_map/ppermute | solution.py:16
  138.4 4.1 %collective-permute-start.20 = (bf16[64,512]{1,0:T(8,128)(2,1)S(1)}, bf16[64,512]{1,0:T(8,128)(2,1)S(1)}, u32[]{:S(2)}, u32[]{:S(2)}) collective-permute-start(bf16[64,512]{1,0:T(8,128)(2,1)S(1)} %fusion.3), channel_id=1, source_target_pairs={{0,16},{4,20},{8,24},{12,28},{16,0},{20,4},{24,8},{28,12},{1,17},{... | collective-permute-start | bytes 196616 | tf_op jit(solution)/shard_map/ppermute | solution.py:16
  142.5 3.4 %collective-permute-start.21 = (bf16[64,512]{1,0:T(8,128)(2,1)S(1)}, bf16[64,512]{1,0:T(8,128)(2,1)S(1)}, u32[]{:S(2)}, u32[]{:S(2)}) collective-permute-start(bf16[64,512]{1,0:T(8,128)(2,1)S(1)} %add_convert_fusion.1), channel_id=1, source_target_pairs={{0,4},{4,0},{8,12},{12,8},{16,20},{20,16},{24,28},{28,24},{1,5},{5... | collective-permute-start | bytes 196616 | tf_op jit(solution)/shard_map/ppermute | solution.py:16
  146.0 5.8 %collective-permute-start.23 = (f32[64]{0:T(128)S(1)}, f32[64]{0:T(128)S(1)}, u32[]{:S(2)}, u32[]{:S(2)}) collective-permute-start(f32[64]{0:T(128)S(1)} %get-tuple-element.31), channel_id=1, source_target_pairs={{0,1},{1,0},{2,3},{3,2},{4,5},{5,4},{6,7},{7,6},{8,9},{9,8},{10,11... | collective-permute-start | bytes 776 | tf_op jit(solution)/shard_map/ppermute | solution.py:16
  155.3 11.8 %collective-permute-start.25 = (bf16[64,4096]{1,0:T(8,128)(2,1)S(1)}, bf16[64,4096]{1,0:T(8,128)(2,1)S(1)}, u32[]{:S(2)}, u32[]{:S(2)}) collective-permute-start(bf16[64,4096]{1,0:T(8,128)(2,1)S(1)} %reduce-precision_convert_fusion), channel_id=1, source_target_pairs={{0,2},{1,3},{2,0},{3,1},{4,6},{5,7},{6,4},{7,5},{8,10},{9,11},{10,... | collective-permute-start | bytes 1572872 | tf_op jit(solution)/shard_map/ppermute | solution.py:16
  167.3 13.2 %collective-permute-start.26 = (bf16[64,4096]{1,0:T(8,128)(2,1)S(1)}, bf16[64,4096]{1,0:T(8,128)(2,1)}, u32[]{:S(2)}, u32[]{:S(2)}) collective-permute-start(bf16[64,4096]{1,0:T(8,128)(2,1)S(1)} %multiply_convert_fusion), channel_id=1, source_target_pairs={{0,1},{1,0},{2,3},{3,2},{4,5},{5,4},{6,7},{7,6},{8,9},{9,8},{10,11... | collective-permute-start | bytes 1572872 | tf_op jit(solution)/shard_map/ppermute | solution.py:16
  (30 other events, 241.1 us)
